TPU v7x, 256 devices: a whole 4x4x8 slice. The times are simulated.
256 devices in a mesh: dp: 32 (over y, z), tensor: 8 (over x, core).
Axes of the slice: x: 4, y: 4, z: 8, core: 2. Of those that a mesh axis runs over, the one named last changes fastest.
Arguments:
- query: bfloat16 [8, 512, 8192], P(None, 'dp', 'tensor'), may hold values from -130 to 130
- new_keys: bfloat16 [8, 512, 1024], P(None, 'dp', 'tensor'), may hold values from -6 to 6
- new_values: bfloat16 [8, 512, 1024], P(None, 'dp', 'tensor'), may hold values from -6 to 6
- cache_keys: bfloat16 [512, 8, 1024, 128], P('dp', 'tensor'), may hold values from -6.5 to 6.5
- cache_values: bfloat16 [512, 8, 1024, 128], P('dp', 'tensor'), may hold values from -6 to 6
- cache_lengths: int32 [512], P('dp'), may hold values from 2 to 1024, as said below
- weight_codes: int32 [8192, 8192], P('tensor', 'dp'), may hold values from -8 to 7
- group_scales: float32 [64, 8192], P('tensor', 'dp'), may hold values from 0.01 to 0.04
Outputs:
- mixed: bfloat16 [8, 512, 8192], P(None, 'tensor', 'dp')
Inputs may be any that keep to these rules, and one draw needn't show every extreme that they name: `cache_lengths`: the requests come in blocks of 16 (the requests of one index of dp); in block g every length is at most 2 + 1022 * (g % 4 + 1) // 4, and the block's first request has exactly that length.
All inputs are finite; a program needn't handle non-finite values.
Results may differ from a plain program's by a relative error of at most 0.015.
Values may be sent and summed in bfloat16 or wider, within the bound.
A program may use at most 128 MiB of HBM per device.

v0:
```python
import jax
import jax.numpy as jnp
from jax import lax
from jax.sharding import PartitionSpec as P

HEADS = 64
KVH = 8
HD = 128
D = 8192
GROUP = 128


def swapped(value, axis, apart):
    mask = 2**apart
    pairs = [(source, source ^ mask) for source in range(lax.axis_size(axis))]
    return lax.ppermute(value, axis, pairs)


def sign_table(order_size):
    line = jnp.arange(order_size, dtype=jnp.int32)
    parity = jnp.zeros((order_size, order_size), jnp.int32)
    for level in range(order_size.bit_length() - 1):
        parity = parity + line[:, None] // 2**level % 2 * (line[None, :] // 2**level % 2)
    return (1 - 2 * (parity % 2)).astype(jnp.float32)


def attend(query, new_keys, new_values, cache_keys, cache_values, cache_lengths):
    steps, req_rows, features = query.shape
    kv_local = cache_keys.shape[1]
    cache_slots = cache_keys.shape[2]
    group_size = HEADS // KVH
    scale = HD ** (-0.5)
    queries = query.reshape(steps, req_rows, kv_local, group_size, HD)
    scores_cache = (
        jnp.einsum("srkgd,rkcd->srkgc", queries, cache_keys, preferred_element_type=jnp.float32)
        * scale
    )
    valid = jnp.arange(cache_slots, dtype=jnp.int32)[None, :] < cache_lengths[:, None]
    scores_cache = jnp.where(valid[None, :, None, None, :], scores_cache, -1e30)
    fresh_keys = new_keys.reshape(steps, req_rows, kv_local, HD)
    scores_new = (
        jnp.einsum("srkgd,trkd->srkgt", queries, fresh_keys, preferred_element_type=jnp.float32)
        * scale
    )
    seen = jnp.arange(steps)[None, :] <= jnp.arange(steps)[:, None]
    scores_new = jnp.where(seen[:, None, None, None, :], scores_new, -1e30)
    peak_score = jnp.maximum(jnp.max(scores_cache, axis=-1), jnp.max(scores_new, axis=-1))[
        ..., None
    ]
    exp_cache = jnp.exp(scores_cache - peak_score)
    exp_new = jnp.exp(scores_new - peak_score)
    total = jnp.sum(exp_cache, axis=-1, keepdims=True) + jnp.sum(exp_new, axis=-1, keepdims=True)
    probs_cache = (exp_cache / total).astype(jnp.bfloat16)
    probs_new = (exp_new / total).astype(jnp.bfloat16)
    fresh_values = new_values.reshape(steps, req_rows, kv_local, HD)
    attended = jnp.einsum(
        "srkgc,rkcd->srkgd", probs_cache, cache_values, preferred_element_type=jnp.float32
    )
    attended = attended + jnp.einsum(
        "srkgt,trkd->srkgd", probs_new, fresh_values, preferred_element_type=jnp.float32
    )
    return attended.astype(jnp.bfloat16).reshape(steps, req_rows, features)


def local_rotate(values):
    steps, req_rows, features = values.shape
    heads_local = features // HD
    blocks = values.reshape(steps, req_rows, heads_local, HD)
    inner = jnp.einsum(
        "srhd,de->srhe",
        blocks,
        sign_table(HD).astype(jnp.bfloat16),
        preferred_element_type=jnp.float32,
    )
    outer = jnp.einsum(
        "gh,srhe->srge", sign_table(heads_local), inner, precision=lax.Precision.HIGHEST
    )
    return outer.reshape(steps, req_rows, features)


def cross_rotate(values):
    width = lax.axis_size("tensor")
    position = lax.axis_index("tensor")
    for level in range(width.bit_length() - 1):
        partner = swapped(values, "tensor", level)
        upper = position // 2**level % 2
        values = jnp.where(upper == 1, partner - values, values + partner)
    return values


def finish_rotation(values):
    return (values * D ** (-0.5)).astype(jnp.bfloat16)


def clip_rows(rotated, peak):
    limit = (0.9 * peak)[..., None]
    return jnp.clip(rotated.astype(jnp.float32), -limit, limit).astype(jnp.bfloat16)


def rotate_and_clip(values):
    rotated = finish_rotation(cross_rotate(local_rotate(values)))
    local_peak = jnp.max(jnp.abs(rotated.astype(jnp.float32)), axis=-1)
    peak = lax.pmax(local_peak, "tensor")
    return clip_rows(rotated, peak)


def body(
    query, new_keys, new_values, cache_keys, cache_values, cache_lengths, weight_codes, group_scales
):
    attended = attend(query, new_keys, new_values, cache_keys, cache_values, cache_lengths)
    rows_local, cols_local = weight_codes.shape
    weight = (
        (
            weight_codes.astype(jnp.float32).reshape(rows_local // GROUP, GROUP, cols_local)
            * group_scales[:, None, :]
        )
        .reshape(rows_local, cols_local)
        .astype(jnp.bfloat16)
    )
    clipped = rotate_and_clip(attended)
    terms = jnp.einsum(
        "srf,fc->src",
        lax.all_gather(clipped, "dp", axis=1, tiled=True),
        weight,
        preferred_element_type=jnp.float32,
    )
    return lax.psum_scatter(terms, "tensor", scatter_dimension=1, tiled=True).astype(jnp.bfloat16)


def solution(mesh):
    return jax.shard_map(
        body,
        mesh=mesh,
        in_specs=(
            P(None, "dp", "tensor"),
            P(None, "dp", "tensor"),
            P(None, "dp", "tensor"),
            P("dp", "tensor", None, None),
            P("dp", "tensor", None, None),
            P("dp"),
            P("tensor", "dp"),
            P("tensor", "dp"),
        ),
        out_specs=P(None, "tensor", "dp"),
        check_vma=False,
    )
```

profile of v0, /device:TPU:1, one launch (start us, length us, event | category | flops | bytes accessed | tf_op | source)
XLA Modules:
  0.0 215.6 jit_solution(8503139035888712571)
XLA Ops:
  6.5 0.0 copy-start
  6.5 0.0 all-gather.2.cloned.1.call-start
  6.6 0.7 iota_compare_fusion
  7.3 1.0 copy.26
  8.3 2.0 fusion.90
  10.4 3.9 %bitcast_reduce_fusion = (f32[8,16,8]{2,0,1:T(8,128)S(1)}, f32[16,1024,8,8]{1,3,2,0:T(8,128)S(1)}) fusion(pred[16,1024]{1,0:T(8,128)(4,1)S(1)} %iota_compare_fusion, bf16[16,1,1024,128]{3,2,1,0:T(8,128)(2,1)} %param.11, bf16[8,16,8,128]{3,2,1,0:T(8,128)(2,1)S(1)} %bitcast.102), kind=kOutput, calls=%fused_computation.5 | convolution fusion | flops 271580160 | bytes 8671232 | tf_op jit(solution)/shard_map/srkgd,rkcd->srkgc/dot_general | solution.py:35
  14.3 0.0 copy-start.3
  14.3 0.2 fusion.21
  14.5 1.2 fusion.5
  15.7 0.8 copy-done.3
  16.4 1.4 fusion
  17.9 0.0 copy-done
  17.9 0.3 fusion.14
  18.2 0.0 copy-start.1
  18.2 0.0 copy-start.2
  18.2 0.4 fusion.23
  18.6 0.6 convolution_bitcast_fusion
  19.3 0.1 reshape.1039
  19.4 3.3 %collective-permute-start = (f32[8,16,1024]{2,1,0:T(8,128)S(1)}, f32[8,16,1024]{2,1,0:T(8,128)S(1)}, u32[]{:S(2)}, u32[]{:S(2)}) collective-permute-start(f32[8,16,1024]{2,1,0:T(8,128)S(1)} %reshape.1039), channel_id=1, source_target_pairs={{0,1},{1,0},{2,3},{3,2},{4,5},{5,4},{6,7},{7,6},{8,9},{9,8},{10,11... | collective-permute-start | bytes 1572872 | tf_op jit(solution)/shard_map/ppermute | solution.py:16
  22.7 1.5 collective-permute-done
  24.2 0.1 add_select_fusion.1
  24.3 0.1 collective-permute-start.1
  24.4 13.1 %collective-permute-done.1 = f32[8,16,1024]{2,1,0:T(8,128)S(1)} collective-permute-done((f32[8,16,1024]{2,1,0:T(8,128)S(1)}, f32[8,16,1024]{2,1,0:T(8,128)S(1)}, u32[]{:S(2)}, u32[]{:S(2)}) %collective-permute-start.1) | collective-permute-done | bytes 524320 | tf_op jit(solution)/shard_map/ppermute | solution.py:16
  37.5 0.1 add_select_fusion
  37.6 1.1 collective-permute-start.2
  38.7 12.7 %collective-permute-done.2 = f32[8,16,1024]{2,1,0:T(8,128)S(1)} collective-permute-done((f32[8,16,1024]{2,1,0:T(8,128)S(1)}, f32[8,16,1024]{2,1,0:T(8,128)S(1)}, u32[]{:S(2)}, u32[]{:S(2)}) %collective-permute-start.2) | collective-permute-done | bytes 524320 | tf_op jit(solution)/shard_map/ppermute | solution.py:16
  51.4 0.2 fusion.16
  51.6 13.9 %pmax.7 = f32[8,16]{1,0:T(8,128)S(1)} all-reduce(f32[8,16]{1,0:T(8,128)S(1)} %get-tuple-element.5), channel_id=1, replica_groups=mesh['dp'=32,'tensor'=8] {'tensor'}, use_global_device_ids=true, to_apply=%region_5.6 | all-reduce | flops 128 | bytes 1024 | tf_op jit(solution)/shard_map/pmax | solution.py:103
  65.5 0.9 fusion.18
  66.4 0.0 all-gather.2.cloned.1.call-update
  66.4 0.0 reduce-scatter.2.cloned.1.call-start
  66.5 0.0 copy-done.1
  66.5 0.0 copy-done.2
  66.5 0.1 fusion.15
  66.6 97.6 %all-gather.2.cloned.1.call-done = bf16[8,512,1024]{2,1,0:T(8,128)(2,1)} async-done(((bf16[8,16,1024]{2,1,0:T(8,128)(2,1)}), bf16[8,512,1024]{2,1,0:T(8,128)(2,1)}) %all-gather.2.cloned.1.call-update) | async-done | bytes 8388624 | tf_op jit(solution)/shard_map/all_gather | solution.py:123
  164.2 7.7 %fusion.19 = f32[8,512,256]{2,1,0:T(8,128)} fusion(bf16[8,512,1024]{2,1,0:T(8,128)(2,1)} %all-gather.2.cloned.1.call-done, bf16[1024,256]{1,0:T(8,128)(2,1)S(1)} %fusion.15), kind=kOutput, calls=%fused_computation.29 | convolution fusion | flops 2147483648 | bytes 13107200 | tf_op jit(solution)/shard_map/srf,fc->src/dot_general | solution.py:121
  171.9 0.0 reduce-scatter.2.cloned.1.call-update
  171.9 35.1 %reduce-scatter.2.cloned.1.call-done = f32[8,64,256]{2,1,0:T(8,128)} async-done(((f32[8,512,256]{2,1,0:T(8,128)}), f32[8,64,256]{2,1,0:T(8,128)}) %reduce-scatter.2.cloned.1.call-update) | async-done | bytes 524304 | tf_op jit(solution)/shard_map/reduce_scatter | solution.py:127
  207.0 1.8 convert_element_type.60
  (10 shorter events, 0.1 us)
Async XLA Ops:
  6.5 11.3 %copy-start = (bf16[8,16,128]{2,1,0:T(8,128)(2,1)S(1)}, bf16[8,16,128]{2,1,0:T(8,128)(2,1)}, u32[]{:S(2)}) copy-start(bf16[8,16,128]{2,1,0:T(8,128)(2,1)} %param.10) | copy-start | bytes 98308
  6.5 157.7 %all-gather.2.cloned.1.call-start = ((), (), s32[]{:S(2)}) async-start(), calls=%async_computation.1 | async-start | bytes 8650752 | tf_op jit(solution)/shard_map/all_gather | solution.py:123
  14.3 2.2 %copy-start.3 = (bf16[16,1,1024,128]{3,2,1,0:T(8,128)(2,1)S(1)}, bf16[16,1,1024,128]{3,2,1,0:T(8,128)(2,1)}, u32[]{:S(2)}) copy-start(bf16[16,1,1024,128]{3,2,1,0:T(8,128)(2,1)} %param.12) | copy-start | bytes 12582916
  18.2 48.3 %copy-start.1 = (s32[1024,256]{1,0:T(8,128)S(1)}, s32[1024,256]{1,0:T(8,128)}, u32[]{:S(2)}) copy-start(s32[1024,256]{1,0:T(8,128)} %param.14) | copy-start | bytes 3145732
  18.2 48.3 %copy-start.2 = (f32[8,256]{1,0:T(8,128)S(1)}, f32[8,256]{1,0:T(8,128)}, u32[]{:S(2)}) copy-start(f32[8,256]{1,0:T(8,128)} %param.15) | copy-start | bytes 24580
  19.4 4.9 %collective-permute-start = (f32[8,16,1024]{2,1,0:T(8,128)S(1)}, f32[8,16,1024]{2,1,0:T(8,128)S(1)}, u32[]{:S(2)}, u32[]{:S(2)}) collective-permute-start(f32[8,16,1024]{2,1,0:T(8,128)S(1)} %reshape.1039), channel_id=1, source_target_pairs={{0,1},{1,0},{2,3},{3,2},{4,5},{5,4},{6,7},{7,6},{8,9},{9,8},{10,11... | collective-permute-start | bytes 1572872 | tf_op jit(solution)/shard_map/ppermute | solution.py:16
  24.3 13.2 %collective-permute-start.1 = (f32[8,16,1024]{2,1,0:T(8,128)S(1)}, f32[8,16,1024]{2,1,0:T(8,128)S(1)}, u32[]{:S(2)}, u32[]{:S(2)}) collective-permute-start(f32[8,16,1024]{2,1,0:T(8,128)S(1)} %add_select_fusion.1), channel_id=1, source_target_pairs={{0,2},{1,3},{2,0},{3,1},{4,6},{5,7},{6,4},{7,5},{8,10},{9,11},{10,... | collective-permute-start | bytes 1572872 | tf_op jit(solution)/shard_map/ppermute | solution.py:16
  37.6 13.8 %collective-permute-start.2 = (f32[8,16,1024]{2,1,0:T(8,128)S(1)}, f32[8,16,1024]{2,1,0:T(8,128)S(1)}, u32[]{:S(2)}, u32[]{:S(2)}) collective-permute-start(f32[8,16,1024]{2,1,0:T(8,128)S(1)} %add_select_fusion), channel_id=1, source_target_pairs={{0,4},{1,5},{2,6},{3,7},{4,0},{5,1},{6,2},{7,3},{8,12},{9,13},{10,... | collective-permute-start | bytes 1572872 | tf_op jit(solution)/shard_map/ppermute | solution.py:16
  66.4 140.6 %reduce-scatter.2.cloned.1.call-start = ((), (), s32[]{:S(2)}) async-start(), calls=%async_computation.2 | async-start | bytes 4718592 | tf_op jit(solution)/shard_map/reduce_scatter | solution.py:127
Sparse Core Ops, SparseCore 0:
  66.6 97.5 all-gather.1
  172.1 34.9 reduce-scatter.1
where the time goes:
time: 218 us; the launch traced here: 216 us
  waiting for transfers between devices  160 us (73%)
  matrix products  16.4 us (8%)
  blocking collectives  13.9 us (6%)
  between operations  13.6 us (6%)
  other arithmetic  5.25 us (2%)
  starting transfers between devices  4.56 us (2%)
    all_gather x1, waiting for transfers between devices, body(): lax.all_gather(clipped, 'dp', axis=1, tiled=True)  97.6 us
    reduce_scatter x1, waiting for transfers between devices, body(): lax.psum_scatter(terms, 'tensor', scatter_dimension=1, tiled=True)  35.1 us
    ppermute x3, waiting for transfers between devices, swapped(): return lax.ppermute(value, axis, pairs)  27.3 us
    pmax x1, blocking collectives, rotate_and_clip(): peak = lax.pmax(local_peak, 'tensor')  13.9 us
    dot_general x1, matrix products, body(): jnp.einsum('srf,fc->src', lax.all_gather(clipped, 'dp', axis=1, tiled=Tru...  7.71 us
    ppermute x3, starting transfers between devices, swapped(): return lax.ppermute(value, axis, pairs)  4.51 us
  transfers between devices with their start and end apart: 5, of which 5 were waited for; matrix products, arithmetic and copies ran while one was open for 0% of the time, Pallas kernels for 0%

commit v1 on v0

v1 whole, which is shorter than its diff:
```python
import functools

import jax
import jax.numpy as jnp
from jax import lax
from jax.experimental import pallas as pl
from jax.experimental.pallas import tpu as pltpu
from jax.sharding import PartitionSpec as P

MESH = pl.DeviceIdType.MESH
HEADS = 64
KVH = 8
HD = 128
D = 8192
GROUP = 128
STEPS = 8
REQ = 16
CACHE = 1024
NX, NY, NZ = 4, 4, 8
LOG2E = 1.4426950408889634
F32 = jnp.float32
BF16 = jnp.bfloat16


def hadamard(size):
    a = lax.broadcasted_iota(jnp.int32, (size, size), 0)
    b = lax.broadcasted_iota(jnp.int32, (size, size), 1)
    bits = a & b
    bits = bits ^ (bits >> 4)
    bits = bits ^ (bits >> 2)
    bits = bits ^ (bits >> 1)
    return (1 - 2 * (bits & 1)).astype(F32)


def butterfly(values):
    span = 1
    while span < len(values):
        out = list(values)
        for at in range(len(values)):
            if at & span == 0:
                out[at] = values[at] + values[at | span]
                out[at | span] = values[at] - values[at | span]
        values = out
        span *= 2
    return values


def kernel(
    lengths,
    q_hbm,
    nk_hbm,
    nv_hbm,
    k_hbm,
    v_hbm,
    codes_hbm,
    scales_hbm,
    out_ref,
    qb,
    nkb,
    nvb,
    kb,
    vb,
    cb,
    sb,
    qf,
    nkf,
    nvf,
    attf,
    att,
    xb,
    rf,
    yb,
    wb,
    ab,
    pb,
    db,
    eb,
    load_sem,
    k_sem,
    v_sem,
    w_send,
    w_recv,
    wc_send,
    wc_recv,
    x_send,
    x_recv,
    y_send,
    y_recv,
    z_send,
    z_recv,
    p_send,
    p_recv,
    e_send,
    e_recv,
):
    dp = lax.axis_index("dp")
    t = lax.axis_index("tensor")
    x, c = t // 2, t % 2
    y, z = dp // NZ, dp % NZ

    def device(dx=0, core=None, dy=0, dz=0):
        at_x = (x + dx) % NX
        at_c = c if core is None else core
        return (((y + dy) % NY) * NZ + (z + dz) % NZ, at_x * 2 + at_c)

    def peer(offset):
        return (dp, (t + offset) % 8)

    def remote(src, dst, send, recv, to):
        return pltpu.make_async_remote_copy(
            src_ref=src, dst_ref=dst, send_sem=send, recv_sem=recv, device_id=to, device_id_type=MESH
        )

    barrier = pltpu.get_barrier_semaphore()
    partners = (
        [peer(offset) for offset in range(1, 8)]
        + [device(dy=dy) for dy in (1, 2, 3)]
        + [device(dz=dz) for dz in (1, NZ - 1)]
    )
    for to in partners:
        pl.semaphore_signal(barrier, inc=1, device_id=to, device_id_type=MESH)

    loads = [
        pltpu.make_async_copy(src, dst, load_sem.at[n])
        for n, (src, dst) in enumerate(
            ((codes_hbm, cb), (scales_hbm, sb), (q_hbm, qb), (nk_hbm, nkb), (nv_hbm, nvb))
        )
    ]

    def load_k(r):
        return pltpu.make_async_copy(k_hbm.at[r, 0], kb.at[r], k_sem.at[r])

    def load_v(r):
        return pltpu.make_async_copy(v_hbm.at[r, 0], vb.at[r], v_sem.at[r])

    for load in loads:
        load.start()

    def start_loads(r, carry):
        load_k(r).start()
        load_v(r).start()
        return carry

    lax.fori_loop(0, REQ, start_loads, 0)

    loads[0].wait()
    loads[1].wait()
    for group in range(8):
        rows = pl.ds(group * GROUP, GROUP)
        wb[c, 0, rows, :] = (cb[rows, :].astype(F32) * sb[group : group + 1, :]).astype(BF16)
    pl.semaphore_wait(barrier, len(partners))

    half_rows = [pl.ds(0, 512), pl.ds(512, 512)]

    def w_copy(n, src_slot, dst_slot, half, dy):
        return remote(
            wb.at[c, src_slot, half_rows[half]],
            wb.at[c, dst_slot, half_rows[half]],
            w_send.at[n],
            w_recv.at[n],
            device(dy=dy),
        )

    w_right = [w_copy(0, 0, 3, 0, 1), w_copy(1, 0, 3, 1, 1)]
    w_left = [w_copy(2, 0, 1, 0, NY - 1), w_copy(3, 0, 1, 1, NY - 1)]
    w_far = [w_copy(4, 3, 2, 0, 1), w_copy(5, 1, 2, 1, NY - 1)]
    w_right[0].start()
    w_left[1].start()
    w_right[1].start()
    w_left[0].start()

    def w_core(slot):
        return remote(
            wb.at[c, slot], wb.at[c, slot], wc_send.at[slot], wc_recv.at[slot], device(core=1 - c)
        )

    w_core(0).start()

    for load in loads[2:]:
        load.wait()
    for s in range(STEPS):
        for g in range(8):
            qf[pl.ds((s * 8 + g) * REQ, REQ), :] = qb[s, :, g * HD : (g + 1) * HD].astype(F32)
        nkf[pl.ds(s * REQ, REQ), :] = nkb[s].astype(F32)
        nvf[pl.ds(s * REQ, REQ), :] = nvb[s].astype(F32)

    slots = lax.broadcasted_iota(jnp.int32, (64, CACHE), 1)
    new_slot = lax.broadcasted_iota(jnp.int32, (64, HD), 1)
    new_step = lax.broadcasted_iota(jnp.int32, (64, HD), 0) // 8
    seen = new_slot <= new_step
    transposed = (((1,), (1,)), ((), ()))
    rate = LOG2E * HD ** (-0.5)

    def attend(r):
        query = jnp.concatenate(
            [qf[pl.ds(i * 8 * REQ + r, 8, stride=REQ), :] for i in range(8)], axis=0
        ).astype(BF16)
        pad = jnp.zeros((HD - STEPS, HD), F32)
        fresh_k = jnp.concatenate([nkf[pl.ds(r, STEPS, stride=REQ), :], pad], axis=0).astype(BF16)
        fresh_v = jnp.concatenate([nvf[pl.ds(r, STEPS, stride=REQ), :], pad], axis=0).astype(BF16)
        load_k(r).wait()
        old = lax.dot_general(query, kb[r], transposed, preferred_element_type=F32)
        new = lax.dot_general(query, fresh_k, transposed, preferred_element_type=F32)
        old = jnp.where(slots < lengths[r], old, -1e30)
        new = jnp.where(seen, new, -1e30)
        peak = jnp.maximum(
            jnp.max(old, axis=1, keepdims=True), jnp.max(new, axis=1, keepdims=True)
        )
        old = jnp.exp2((old - peak) * rate)
        new = jnp.exp2((new - peak) * rate)
        total = jnp.sum(old, axis=1, keepdims=True) + jnp.sum(new, axis=1, keepdims=True)
        load_v(r).wait()
        result = jnp.dot(old.astype(BF16), vb[r], preferred_element_type=F32)
        result = result + jnp.dot(new.astype(BF16), fresh_v, preferred_element_type=F32)
        result = result / total
        for i in range(8):
            attf[pl.ds(i * 8 * REQ + r, 8, stride=REQ), :] = result[i * 8 : (i + 1) * 8, :]

    def attend_two(n, carry):
        attend(2 * n)
        attend(2 * n + 1)
        return carry

    lax.fori_loop(0, REQ // 2, attend_two, 0)

    for s in range(STEPS):
        for g in range(8):
            att[s, :, g * HD : (g + 1) * HD] = attf[pl.ds((s * 8 + g) * REQ, REQ), :].astype(BF16)

    def x_copy(offset):
        to = peer(offset)
        return remote(att.at[to[1]], xb.at[t], x_send.at[offset], x_recv.at[offset], to)

    for offset in (4, 3, 5, 2, 6, 1, 7):
        x_copy(offset).start()
    xb[t] = att[t]

    w_right[0].wait_recv()
    w_far[0].start()
    w_left[1].wait_recv()
    w_far[1].start()

    for offset in range(1, 8):
        x_copy(offset).wait_recv()

    signs = hadamard(HD).astype(BF16)
    for g in range(8):
        heads = xb[:, :, g * HD : (g + 1) * HD].reshape(8 * REQ, HD)
        rf[g] = jnp.dot(heads, signs, preferred_element_type=F32)
    for kv in range(8):
        rows = pl.ds(kv * REQ, REQ)
        for g, value in enumerate(butterfly([rf[g, rows, :] for g in range(8)])):
            rf[g, rows, :] = value
    top = jnp.zeros((REQ, HD), F32)
    for g in range(8):
        values = butterfly([rf[g, pl.ds(kv * REQ, REQ), :] for kv in range(8)])
        for kv, value in enumerate(values):
            value = (value * D ** (-0.5)).astype(BF16)
            yb[kv // 2, kv % 2, :, g * HD : (g + 1) * HD] = value
            top = jnp.maximum(top, jnp.abs(value.astype(F32)))
    limit = 0.9 * jnp.max(top, axis=1, keepdims=True)
    for kv in range(8):
        value = yb[kv // 2, kv % 2].astype(F32)
        yb[kv // 2, kv % 2] = jnp.clip(value, -limit, limit).astype(BF16)

    row_core = t // 4
    row_slot = t % 4

    def y_copy(dx):
        return remote(
            yb.at[(x + dx) % NX],
            ab.at[0, row_slot],
            y_send.at[dx],
            y_recv.at[row_slot],
            device(dx=dx, core=row_core),
        )

    def y_local():
        return pltpu.make_async_copy(yb.at[x], ab.at[0, row_slot], y_recv.at[row_slot])

    for dx in (2, 1, 3):
        y_copy(dx).start()

    @pl.when(row_core == c)
    def _():
        y_local().start()

    @pl.when(row_core != c)
    def _():
        y_copy(0).start()

    def y_arrived(slot):
        pltpu.make_async_copy(yb.at[0], ab.at[0, slot], y_recv.at[slot]).wait()

    def z_copy(way, d, half):
        src = 0 if d == 1 else (2 * (d - 1) - 1 if way == 0 else 2 * (d - 1))
        dst = 7 if d == 4 else (2 * d - 1 if way == 0 else 2 * d)
        rows = pl.ds(2 * half, 2)
        return remote(
            ab.at[src, rows],
            ab.at[dst, rows],
            z_send.at[way, d - 1, half],
            z_recv.at[way, d - 1, half],
            device(dz=1 if way == 0 else NZ - 1),
        )

    first = [0, 1]

    y_arrived(0)
    y_arrived(1)
    z_copy(0, 1, 0).start()
    z_copy(1, 1, 0).start()
    y_arrived(2)
    y_arrived(3)
    z_copy(0, 1, 1).start()
    z_copy(1, 1, 1).start()

    w_right[1].wait_recv()
    w_core(3).start()
    w_left[0].wait_recv()
    w_core(1).start()
    w_far[0].wait_recv()
    w_far[1].wait_recv()
    w_core(2).start()
    w_core(0).wait_recv()

    spans = [(0, 1), (1, 3), (3, 5), (5, 7), (7, 8)]

    def project(stage, i):
        lo, hi = spans[stage]
        rows = (hi - lo) * 64
        total = jnp.zeros((rows, 256), F32)
        for core in range(2):
            block = ab[lo:hi, :, core].reshape(rows, 1024)
            total = total + jnp.dot(block, wb[core, i], preferred_element_type=F32)
        total = total.astype(BF16).reshape(hi - lo, 64, 256)
        if i == 0:
            db[0, lo:hi] = total
        else:
            pb[i, lo:hi] = total

    def p_copy(stage, i):
        lo, hi = spans[stage]
        at = pl.ds(lo, hi - lo)
        return remote(
            pb.at[i, at], db.at[i, at], p_send.at[stage, i], p_recv.at[stage, i], device(dy=i)
        )

    def z_of(pos):
        dz = 4 if pos == 7 else (NZ - (pos + 1) // 2 if pos % 2 else pos // 2)
        return (z + dz) % NZ

    def e_copy(pos, k):
        block = z_of(pos)
        to_x = (x + k) % NX
        i = (y + NY - to_x) % NY
        return remote(
            db.at[i, pos],
            eb.at[k, c, block % 4],
            e_send.at[k, pos],
            e_recv.at[k, c, block % 4],
            device(dx=k, core=block // 4),
        )

    def e_local(pos):
        block = z_of(pos)
        i = (y + NY - x) % NY
        return pltpu.make_async_copy(
            db.at[i, pos], eb.at[0, c, block % 4], e_recv.at[0, c, block % 4]
        )

    def forward(stage):
        for i in (1, 2, 3):
            p_copy(stage, i).wait_recv()
        for pos in range(*spans[stage]):
            for k in (2, 1, 3):
                e_copy(pos, k).start()
            own = z_of(pos) // 4 == c

            @pl.when(own)
            def _():
                e_local(pos).start()

            @pl.when(jnp.logical_not(own))
            def _():
                e_copy(pos, 0).start()

    for stage in range(5):
        if stage:
            if stage < 4:
                for half in first:
                    for way in range(2):
                        z_copy(way, stage, half).wait_recv()
                        if stage < 3 or half == way:
                            z_copy(way, stage + 1, half).start()
            else:
                z_copy(0, 4, 0).wait_recv()
                z_copy(1, 4, 1).wait_recv()
        for i in (1, 3, 2, 0):
            if stage == 0 and i:
                w_core(i).wait_recv()
            project(stage, i)
            if i:
                p_copy(stage, i).start()
        if stage:
            forward(stage - 1)
    forward(4)

    for zz in range(4):
        for core in range(2):
            for k in range(4):
                pltpu.make_async_copy(
                    db.at[0, 0], eb.at[k, core, zz], e_recv.at[k, core, zz]
                ).wait()
            total = eb[0, core, zz].astype(F32)
            for k in range(1, 4):
                total = total + eb[k, core, zz].astype(F32)
            out_ref[4 * core : 4 * core + 4, zz * REQ : (zz + 1) * REQ, :] = total.astype(
                BF16
            ).reshape(4, REQ, 256)

    for copy in w_right + w_left + w_far:
        copy.wait_send()
    for slot in range(4):
        w_core(slot).wait_send()
    for offset in range(1, 8):
        x_copy(offset).wait_send()
    for dx in (1, 2, 3):
        y_copy(dx).wait_send()

    @pl.when(row_core != c)
    def _():
        y_copy(0).wait_send()

    for d in range(1, 5):
        for half in range(2):
            for way in range(2):
                if d < 4 or half == way:
                    z_copy(way, d, half).wait_send()
    for stage in range(5):
        for i in (1, 2, 3):
            p_copy(stage, i).wait_send()
    for pos in range(8):
        for k in (1, 2, 3):
            e_copy(pos, k).wait_send()

        @pl.when(z_of(pos) // 4 != c)
        def _():
            e_copy(pos, 0).wait_send()


def body(
    query, new_keys, new_values, cache_keys, cache_values, cache_lengths, weight_codes, group_scales
):
    hbm = pl.BlockSpec(memory_space=pl.ANY)
    dma = pltpu.SemaphoreType.DMA
    return pl.pallas_call(
        kernel,
        out_shape=jax.ShapeDtypeStruct((STEPS, 64, 256), BF16),
        in_specs=[pl.BlockSpec(memory_space=pltpu.SMEM)] + [hbm] * 7,
        out_specs=pl.BlockSpec(memory_space=pltpu.VMEM),
        scratch_shapes=[
            pltpu.VMEM((STEPS, REQ, 1024), BF16),
            pltpu.VMEM((STEPS, REQ, HD), BF16),
            pltpu.VMEM((STEPS, REQ, HD), BF16),
            pltpu.VMEM((REQ, CACHE, HD), BF16),
            pltpu.VMEM((REQ, CACHE, HD), BF16),
            pltpu.VMEM((1024, 256), jnp.int32),
            pltpu.VMEM((8, 256), F32),
            pltpu.VMEM((64 * REQ, HD), F32),
            pltpu.VMEM((STEPS * REQ, HD), F32),
            pltpu.VMEM((STEPS * REQ, HD), F32),
            pltpu.VMEM((64 * REQ, HD), F32),
            pltpu.VMEM((STEPS, REQ, 1024), BF16),
            pltpu.VMEM((8, REQ, 1024), BF16),
            pltpu.VMEM((8, 8 * REQ, HD), F32),
            pltpu.VMEM((NX, 2, REQ, 1024), BF16),
            pltpu.VMEM((2, NY, 1024, 256), BF16),
            pltpu.VMEM((8, 4, 2, REQ, 1024), BF16),
            pltpu.VMEM((NY, 8, 64, 256), BF16),
            pltpu.VMEM((NY, 8, 64, 256), BF16),
            pltpu.VMEM((NX, 2, 4, 64, 256), BF16),
            dma((5,)),
            dma((REQ,)),
            dma((REQ,)),
            dma((6,)),
            dma((6,)),
            dma((4,)),
            dma((4,)),
            dma((8,)),
            dma((8,)),
            dma((4,)),
            dma((4,)),
            dma((2, 4, 2)),
            dma((2, 4, 2)),
            dma((5, 4)),
            dma((5, 4)),
            dma((NX, 8)),
            dma((NX, 2, 4)),
        ],
        compiler_params=pltpu.CompilerParams(
            collective_id=0, has_side_effects=True, vmem_limit_bytes=48 << 20
        ),
        name="decode",
    )(
        cache_lengths,
        query,
        new_keys,
        new_values,
        cache_keys,
        cache_values,
        weight_codes,
        group_scales,
    )


def solution(mesh):
    return jax.shard_map(
        body,
        mesh=mesh,
        in_specs=(
            P(None, "dp", "tensor"),
            P(None, "dp", "tensor"),
            P(None, "dp", "tensor"),
            P("dp", "tensor", None, None),
            P("dp", "tensor", None, None),
            P("dp"),
            P("tensor", "dp"),
            P("tensor", "dp"),
        ),
        out_specs=P(None, "tensor", "dp"),
        check_vma=False,
    )
```

time: 218 us -> 73 us (0.33)
  waiting for transfers between devices: 160 us -> 0 us
  Pallas kernels: 0 us -> 64.7 us
  matrix products: 16.4 us -> 0 us
  blocking collectives: 13.9 us -> 0 us
  between operations: 13.6 us -> 0.02 us
  local copies, waits for them, and re-layouts: 1.87 us -> 7.93 us
  other arithmetic: 5.25 us -> 0 us
  starting transfers between devices: 4.56 us -> 0 us
    all_gather x1 -> x0, waiting for transfers between devices: 97.6 us -> none  [body(): lax.all_gather(clipped, 'dp', axis=1, tiled=True)]
    pallas_call x0 -> x1, Pallas kernels: none -> 64.7 us  [body(): pl.pallas_call(kernel, out_shape=jax.ShapeDtypeStruct((STEPS, 64, 256), B...]
    reduce_scatter x1 -> x0, waiting for transfers between devices: 35.1 us -> none  [body(): lax.psum_scatter(terms, 'tensor', scatter_dimension=1, tiled=True)]
    ppermute x3 -> x0, waiting for transfers between devices: 27.3 us -> none  [swapped(): return lax.ppermute(value, axis, pairs)]
    dot_general x7 -> x0, matrix products: 16.4 us -> none  [the longest x1 7.71 us: body(): jnp.einsum('srf,fc->src', lax.all_gather(clipped, 'dp', axis=1, tiled=Tru...]
    pmax x1 -> x0, blocking collectives: 13.9 us -> none  [rotate_and_clip(): peak = lax.pmax(local_peak, 'tensor')]
    unnamed x9 -> x15, local copies, waits for them, and re-layouts: 1.79 us -> 7.93 us
    ppermute x3 -> x0, starting transfers between devices: 4.51 us -> none  [swapped(): return lax.ppermute(value, axis, pairs)]
  transfers between devices with their start and end apart: 5 -> 0, of which waited for: 5 -> 0; matrix products, arithmetic and copies ran while one was open for 0% -> 0% of each run, Pallas kernels for 0% -> 0%
where the time goes in v1:
time: 73 us; the launch traced here: 72.6 us
  Pallas kernels  64.7 us (89%)
  local copies, waits for them, and re-layouts  7.93 us (11%)
    pallas_call x1, Pallas kernels, body(): pl.pallas_call(kernel, out_shape=jax.ShapeDtypeStruct((STEPS, 64, 256), B...  64.7 us
    unnamed x15, local copies, waits for them, and re-layouts  7.93 us

profile of v1, /device:TPU:1, one launch (start us, length us, event | category | flops | bytes accessed | tf_op | source)
XLA Modules:
  0.0 72.6 jit_solution(5824411055795967502)
XLA Ops:
  0.0 0.0 copy-start
  0.0 2.2 %copy-done = bf16[16,1,1024,128]{3,2,1,0:T(8,128)(2,1)S(1)} copy-done((bf16[16,1,1024,128]{3,2,1,0:T(8,128)(2,1)S(1)}, bf16[16,1,1024,128]{3,2,1,0:T(8,128)(2,1)}, u32[]{:S(2)}) %copy-start) | copy-done | bytes 4194328
  2.2 0.0 copy-start.1
  2.2 1.2 %copy-done.1 = s32[1024,256]{1,0:T(8,128)S(1)} copy-done((s32[1024,256]{1,0:T(8,128)S(1)}, s32[1024,256]{1,0:T(8,128)}, u32[]{:S(2)}) %copy-start.1) | copy-done | bytes 1048600
  3.4 0.0 copy-start.2
  3.4 0.9 %copy-done.2 = bf16[8,16,1024]{2,1,0:T(8,128)(2,1)S(1)} copy-done((bf16[8,16,1024]{2,1,0:T(8,128)(2,1)S(1)}, bf16[8,16,1024]{2,1,0:T(8,128)(2,1)}, u32[]{:S(2)}) %copy-start.2) | copy-done | bytes 262168
  4.4 0.0 copy-start.3
  4.4 0.8 %copy-done.3 = bf16[8,16,128]{2,1,0:T(8,128)(2,1)S(1)} copy-done((bf16[8,16,128]{2,1,0:T(8,128)(2,1)S(1)}, bf16[8,16,128]{2,1,0:T(8,128)(2,1)}, u32[]{:S(2)}) %copy-start.3) | copy-done | bytes 32792
  5.1 0.0 copy-start.4
  5.1 0.8 %copy-done.4 = bf16[8,16,128]{2,1,0:T(8,128)(2,1)S(1)} copy-done((bf16[8,16,128]{2,1,0:T(8,128)(2,1)S(1)}, bf16[8,16,128]{2,1,0:T(8,128)(2,1)}, u32[]{:S(2)}) %copy-start.4) | copy-done | bytes 32792
  5.9 0.0 copy-start.5
  5.9 0.7 copy-done.5
  6.6 0.0 copy-start.6
  6.6 0.7 copy-done.6
  7.2 64.7 %decode.1 = bf16[8,64,256]{2,1,0:T(8,128)(2,1)S(1)} custom-call(s32[16]{0:T(128)S(1)} %copy-done.6, bf16[8,16,1024]{2,1,0:T(8,128)(2,1)S(1)} %copy-done.2, bf16[8,16,128]{2,1,0:T(8,128)(2,1)S(1)} %copy-done.3, bf16[8,16,128]{2,1,0:T(8,128)(2,1)S(1)} %copy-done.4, bf16[16,1,1024,128]{3,2,1,0:T(8,128)(2,1)S(1)} %copy-done, bf16[16,1,1024,128]{3,2,1,0:T(8,128)(2,1)} %v_hbm.1, ...), custom_call_target="tpu_custom_call" | custom-call | tf_op jit(solution)/shard_map/decode/pallas_call | solution.py:457
  71.9 0.7 copy.10
Async XLA Ops:
  0.0 2.2 %copy-start = (bf16[16,1,1024,128]{3,2,1,0:T(8,128)(2,1)S(1)}, bf16[16,1,1024,128]{3,2,1,0:T(8,128)(2,1)}, u32[]{:S(2)}) copy-start(bf16[16,1,1024,128]{3,2,1,0:T(8,128)(2,1)} %k_hbm.1) | copy-start | bytes 12582916
  2.2 1.2 %copy-start.1 = (s32[1024,256]{1,0:T(8,128)S(1)}, s32[1024,256]{1,0:T(8,128)}, u32[]{:S(2)}) copy-start(s32[1024,256]{1,0:T(8,128)} %codes_hbm.1) | copy-start | bytes 3145732
  3.4 0.9 %copy-start.2 = (bf16[8,16,1024]{2,1,0:T(8,128)(2,1)S(1)}, bf16[8,16,1024]{2,1,0:T(8,128)(2,1)}, u32[]{:S(2)}) copy-start(bf16[8,16,1024]{2,1,0:T(8,128)(2,1)} %q_hbm.1) | copy-start | bytes 786436
  4.4 0.8 %copy-start.3 = (bf16[8,16,128]{2,1,0:T(8,128)(2,1)S(1)}, bf16[8,16,128]{2,1,0:T(8,128)(2,1)}, u32[]{:S(2)}) copy-start(bf16[8,16,128]{2,1,0:T(8,128)(2,1)} %nk_hbm.1) | copy-start | bytes 98308
  5.1 0.8 %copy-start.4 = (bf16[8,16,128]{2,1,0:T(8,128)(2,1)S(1)}, bf16[8,16,128]{2,1,0:T(8,128)(2,1)}, u32[]{:S(2)}) copy-start(bf16[8,16,128]{2,1,0:T(8,128)(2,1)} %nv_hbm.1) | copy-start | bytes 98308
  5.9 0.7 copy-start.5
  6.6 0.7 copy-start.6

commit v2 on v1

--- a/solution.py
+++ b/solution.py
@@ -17,6 +17,7 @@
 REQ = 16
 CACHE = 1024
 NX, NY, NZ = 4, 4, 8
+GROUPED = 4
 LOG2E = 1.4426950408889634
 F32 = jnp.float32
 BF16 = jnp.bfloat16
@@ -191,57 +192,87 @@
     transposed = (((1,), (1,)), ((), ()))
     rate = LOG2E * HD ** (-0.5)
 
-    def attend(r):
-        query = jnp.concatenate(
-            [qf[pl.ds(i * 8 * REQ + r, 8, stride=REQ), :] for i in range(8)], axis=0
-        ).astype(BF16)
+    def attend(first, count):
+        group = [first + n for n in range(count)]
+        for r in group:
+            load_k(r).wait()
+            load_v(r).wait()
         pad = jnp.zeros((HD - STEPS, HD), F32)
-        fresh_k = jnp.concatenate([nkf[pl.ds(r, STEPS, stride=REQ), :], pad], axis=0).astype(BF16)
-        fresh_v = jnp.concatenate([nvf[pl.ds(r, STEPS, stride=REQ), :], pad], axis=0).astype(BF16)
-        load_k(r).wait()
-        old = lax.dot_general(query, kb[r], transposed, preferred_element_type=F32)
-        new = lax.dot_general(query, fresh_k, transposed, preferred_element_type=F32)
-        old = jnp.where(slots < lengths[r], old, -1e30)
-        new = jnp.where(seen, new, -1e30)
-        peak = jnp.maximum(
-            jnp.max(old, axis=1, keepdims=True), jnp.max(new, axis=1, keepdims=True)
-        )
-        old = jnp.exp2((old - peak) * rate)
-        new = jnp.exp2((new - peak) * rate)
-        total = jnp.sum(old, axis=1, keepdims=True) + jnp.sum(new, axis=1, keepdims=True)
-        load_v(r).wait()
-        result = jnp.dot(old.astype(BF16), vb[r], preferred_element_type=F32)
-        result = result + jnp.dot(new.astype(BF16), fresh_v, preferred_element_type=F32)
-        result = result / total
-        for i in range(8):
-            attf[pl.ds(i * 8 * REQ + r, 8, stride=REQ), :] = result[i * 8 : (i + 1) * 8, :]
-
-    def attend_two(n, carry):
-        attend(2 * n)
-        attend(2 * n + 1)
+        queries = [
+            jnp.concatenate(
+                [qf[pl.ds(i * 8 * REQ + r, 8, stride=REQ), :] for i in range(8)], axis=0
+            ).astype(BF16)
+            for r in group
+        ]
+        fresh_k, fresh_v = (
+            [
+                jnp.concatenate([ref[pl.ds(r, STEPS, stride=REQ), :], pad], axis=0).astype(BF16)
+                for r in group
+            ]
+            for ref in (nkf, nvf)
+        )
+        olds = [
+            lax.dot_general(query, kb[r], transposed, preferred_element_type=F32)
+            for query, r in zip(queries, group)
+        ]
+        news = [
+            lax.dot_general(query, fresh, transposed, preferred_element_type=F32)
+            for query, fresh in zip(queries, fresh_k)
+        ]
+        results = []
+        for n, r in enumerate(group):
+            old = jnp.where(slots < lengths[r], olds[n], -1e30)
+            new = jnp.where(seen, news[n], -1e30)
+            peak = jnp.maximum(
+                jnp.max(old, axis=1, keepdims=True), jnp.max(new, axis=1, keepdims=True)
+            )
+            old = jnp.exp2((old - peak) * rate)
+            new = jnp.exp2((new - peak) * rate)
+            total = jnp.sum(old, axis=1, keepdims=True) + jnp.sum(new, axis=1, keepdims=True)
+            result = jnp.dot(old.astype(BF16), vb[r], preferred_element_type=F32)
+            result = result + jnp.dot(new.astype(BF16), fresh_v[n], preferred_element_type=F32)
+            results.append(result / total)
+        for r, result in zip(group, results):
+            for i in range(8):
+                start = (i // 2) * 8 * REQ + (i % 2) * 8 + r % 8
+                attf[r // 8, pl.ds(start, 8, stride=REQ), :] = result[i * 8 : (i + 1) * 8, :]
+
+    def attend_some(n, carry):
+        attend(GROUPED * n, GROUPED)
         return carry
 
-    lax.fori_loop(0, REQ // 2, attend_two, 0)
-
-    for s in range(STEPS):
-        for g in range(8):
-            att[s, :, g * HD : (g + 1) * HD] = attf[pl.ds((s * 8 + g) * REQ, REQ), :].astype(BF16)
-
-    def x_copy(offset):
-        to = peer(offset)
-        return remote(att.at[to[1]], xb.at[t], x_send.at[offset], x_recv.at[offset], to)
-
-    for offset in (4, 3, 5, 2, 6, 1, 7):
-        x_copy(offset).start()
-    xb[t] = att[t]
+    def x_copy(q, offset):
+        to = q * 4 + (t + offset) % 4
+        return remote(att.at[to], xb.at[t], x_send.at[q, offset], x_recv.at[t], (dp, to))
+
+    def x_local():
+        return pltpu.make_async_copy(att.at[t], xb.at[t], x_recv.at[t])
+
+    for q in range(2):
+        lax.fori_loop(q * 8 // GROUPED, (q + 1) * 8 // GROUPED, attend_some, 0)
+        for u in range(4):
+            for g in range(8):
+                att[q * 4 + u, :, g * HD : (g + 1) * HD] = attf[
+                    q, pl.ds((u * 8 + g) * REQ, REQ), :
+                ].astype(BF16)
+        for offset in (2, 1, 3):
+            x_copy(q, offset).start()
+
+        @pl.when(t // 4 == q)
+        def _():
+            x_local().start()
+
+        @pl.when(t // 4 != q)
+        def _():
+            x_copy(q, 0).start()
 
     w_right[0].wait_recv()
     w_far[0].start()
     w_left[1].wait_recv()
     w_far[1].start()
 
-    for offset in range(1, 8):
-        x_copy(offset).wait_recv()
+    for source in range(8):
+        pltpu.make_async_copy(att.at[0], xb.at[source], x_recv.at[source]).wait()
 
     signs = hadamard(HD).astype(BF16)
     for g in range(8):
@@ -263,31 +294,14 @@
         value = yb[kv // 2, kv % 2].astype(F32)
         yb[kv // 2, kv % 2] = jnp.clip(value, -limit, limit).astype(BF16)
 
-    row_core = t // 4
-    row_slot = t % 4
-
     def y_copy(dx):
         return remote(
-            yb.at[(x + dx) % NX],
-            ab.at[0, row_slot],
-            y_send.at[dx],
-            y_recv.at[row_slot],
-            device(dx=dx, core=row_core),
-        )
-
-    def y_local():
-        return pltpu.make_async_copy(yb.at[x], ab.at[0, row_slot], y_recv.at[row_slot])
+            yb.at[(x + dx) % NX], ab.at[0, x], y_send.at[dx], y_recv.at[x], device(dx=dx)
+        )
 
     for dx in (2, 1, 3):
         y_copy(dx).start()
-
-    @pl.when(row_core == c)
-    def _():
-        y_local().start()
-
-    @pl.when(row_core != c)
-    def _():
-        y_copy(0).start()
+    pltpu.make_async_copy(yb.at[x], ab.at[0, x], y_recv.at[x]).start()
 
     def y_arrived(slot):
         pltpu.make_async_copy(yb.at[0], ab.at[0, slot], y_recv.at[slot]).wait()
@@ -304,25 +318,11 @@
             device(dz=1 if way == 0 else NZ - 1),
         )
 
-    first = [0, 1]
-
-    y_arrived(0)
-    y_arrived(1)
-    z_copy(0, 1, 0).start()
-    z_copy(1, 1, 0).start()
-    y_arrived(2)
-    y_arrived(3)
-    z_copy(0, 1, 1).start()
-    z_copy(1, 1, 1).start()
-
-    w_right[1].wait_recv()
-    w_core(3).start()
-    w_left[0].wait_recv()
-    w_core(1).start()
-    w_far[0].wait_recv()
-    w_far[1].wait_recv()
-    w_core(2).start()
-    w_core(0).wait_recv()
+    def z_first(half):
+        y_arrived(2 * half)
+        y_arrived(2 * half + 1)
+        z_copy(0, 1, half).start()
+        z_copy(1, 1, half).start()
 
     spans = [(0, 1), (1, 3), (3, 5), (5, 7), (7, 8)]
 
@@ -385,52 +385,82 @@
             def _():
                 e_copy(pos, 0).start()
 
-    for stage in range(5):
-        if stage:
-            if stage < 4:
-                for half in first:
-                    for way in range(2):
-                        z_copy(way, stage, half).wait_recv()
-                        if stage < 3 or half == way:
-                            z_copy(way, stage + 1, half).start()
-            else:
-                z_copy(0, 4, 0).wait_recv()
-                z_copy(1, 4, 1).wait_recv()
+    def pass_on(d, half):
+        for way in range(2):
+            z_copy(way, d, half).wait_recv()
+            if d < 3 or half == way:
+                z_copy(way, d + 1, half).start()
+
+    def multiply(stage):
         for i in (1, 3, 2, 0):
             if stage == 0 and i:
                 w_core(i).wait_recv()
             project(stage, i)
             if i:
                 p_copy(stage, i).start()
-        if stage:
-            forward(stage - 1)
+
+    z_first(0)
+    w_right[1].wait_recv()
+    w_core(3).start()
+    w_left[0].wait_recv()
+    w_core(1).start()
+    z_first(1)
+    pass_on(1, 0)
+    w_far[0].wait_recv()
+    w_far[1].wait_recv()
+    w_core(2).start()
+    pass_on(1, 1)
+    w_core(0).wait_recv()
+    multiply(0)
+    pass_on(2, 0)
+    multiply(1)
+    pass_on(2, 1)
+    forward(0)
+    pass_on(3, 0)
+    multiply(2)
+    forward(1)
+    pass_on(3, 1)
+    multiply(3)
+    forward(2)
+    z_copy(0, 4, 0).wait_recv()
+    z_copy(1, 4, 1).wait_recv()
+    multiply(4)
+    forward(3)
     forward(4)
 
-    for zz in range(4):
+    for n in range(1, 5):
+        zz = (z + n) % 4
+        rows = pl.ds(pl.multiple_of(zz * REQ, REQ), REQ)
         for core in range(2):
             for k in range(4):
                 pltpu.make_async_copy(
                     db.at[0, 0], eb.at[k, core, zz], e_recv.at[k, core, zz]
                 ).wait()
+        for core in range(2):
             total = eb[0, core, zz].astype(F32)
             for k in range(1, 4):
                 total = total + eb[k, core, zz].astype(F32)
-            out_ref[4 * core : 4 * core + 4, zz * REQ : (zz + 1) * REQ, :] = total.astype(
-                BF16
-            ).reshape(4, REQ, 256)
+            for pair in range(2):
+                for step in range(2):
+                    parts = [total[at : at + 8] for at in (pair * 16 + step * 8, 32 + pair * 16 + step * 8)]
+                    out_ref[4 * pair + 2 * core + step, rows, :] = (
+                        jnp.concatenate(parts, axis=0).astype(BF16)
+                    )
 
     for copy in w_right + w_left + w_far:
         copy.wait_send()
     for slot in range(4):
         w_core(slot).wait_send()
-    for offset in range(1, 8):
-        x_copy(offset).wait_send()
+    for q in range(2):
+        for offset in (1, 2, 3):
+            x_copy(q, offset).wait_send()
+
+        @pl.when(t // 4 != q)
+        def _():
+            x_copy(q, 0).wait_send()
+
     for dx in (1, 2, 3):
         y_copy(dx).wait_send()
-
-    @pl.when(row_core != c)
-    def _():
-        y_copy(0).wait_send()
 
     for d in range(1, 5):
         for half in range(2):
@@ -470,8 +500,8 @@
             pltpu.VMEM((64 * REQ, HD), F32),
             pltpu.VMEM((STEPS * REQ, HD), F32),
             pltpu.VMEM((STEPS * REQ, HD), F32),
-            pltpu.VMEM((64 * REQ, HD), F32),
-            pltpu.VMEM((STEPS, REQ, 1024), BF16),
+            pltpu.VMEM((2, 32 * REQ, HD), F32),
+            pltpu.VMEM((8, REQ, 1024), BF16),
             pltpu.VMEM((8, REQ, 1024), BF16),
             pltpu.VMEM((8, 8 * REQ, HD), F32),
             pltpu.VMEM((NX, 2, REQ, 1024), BF16),
@@ -487,7 +517,7 @@
             dma((6,)),
             dma((4,)),
             dma((4,)),
-            dma((8,)),
+            dma((2, 4)),
             dma((8,)),
             dma((4,)),
             dma((4,)),
@@ -499,7 +529,7 @@
             dma((NX, 2, 4)),
         ],
         compiler_params=pltpu.CompilerParams(
-            collective_id=0, has_side_effects=True, vmem_limit_bytes=48 << 20
+            collective_id=0, has_side_effects=True, vmem_limit_bytes=60 << 20
         ),
         name="decode",
     )(

time: 73 us -> 59.7 us (0.82)
  Pallas kernels: 64.7 us -> 57.9 us
  local copies, waits for them, and re-layouts: 7.93 us -> 1.67 us
    pallas_call x1, Pallas kernels: 64.7 us -> 57.9 us  [body(): pl.pallas_call(kernel, out_shape=jax.ShapeDtypeStruct((STEPS, 64, 256), B...]
    unnamed x15 -> x1, local copies, waits for them, and re-layouts: 7.93 us -> 1.67 us
where the time goes in v2:
time: 59.7 us; the launch traced here: 59.5 us
  Pallas kernels  57.9 us (97%)
  local copies, waits for them, and re-layouts  1.67 us (3%)
    pallas_call x1, Pallas kernels, body(): pl.pallas_call(kernel, out_shape=jax.ShapeDtypeStruct((STEPS, 64, 256), B...  57.9 us
    unnamed x1, local copies, waits for them, and re-layouts  1.67 us

profile of v2, /device:TPU:1, one launch (start us, length us, event | category | flops | bytes accessed | tf_op | source)
XLA Modules:
  0.0 59.5 jit_solution(6814714796901671342)
XLA Ops:
  0.0 57.9 %decode.1 = bf16[8,64,256]{2,1,0:T(8,128)(2,1)} custom-call(s32[16]{0:T(128)} %lengths.1, bf16[8,16,1024]{2,1,0:T(8,128)(2,1)} %q_hbm.1, bf16[8,16,128]{2,1,0:T(8,128)(2,1)} %nk_hbm.1, bf16[8,16,128]{2,1,0:T(8,128)(2,1)} %nv_hbm.1, bf16[16,1,1024,128]{3,2,1,0:T(8,128)(2,1)} %k_hbm.1, bf16[16,1,1024,128]{3,2,1,0:T(8,128)(2,1)} %v_hbm.1, ...), custom_call_target="tpu_custom_call" | custom-call | tf_op jit(solution)/shard_map/decode/pallas_call | solution.py:487
  57.9 1.7 %copy.10 = bf16[8,64,256]{2,1,0:T(8,128)(2,1)} copy(bf16[8,64,256]{2,1,0:T(8,128)(2,1)} %decode.1) | data formatting | bytes 524288

commit v3 on v2

--- a/solution.py
+++ b/solution.py
@@ -76,6 +76,7 @@
     pb,
     db,
     eb,
+    outf,
     load_sem,
     k_sem,
     v_sem,
@@ -142,7 +143,6 @@
         load_v(r).start()
         return carry
 
-    lax.fori_loop(0, REQ, start_loads, 0)
 
     loads[0].wait()
     loads[1].wait()
@@ -176,6 +176,7 @@
         )
 
     w_core(0).start()
+    lax.fori_loop(0, REQ, start_loads, 0)
 
     for load in loads[2:]:
         load.wait()
@@ -242,7 +243,7 @@
         return carry
 
     def x_copy(q, offset):
-        to = q * 4 + (t + offset) % 4
+        to = 2 * ((x + offset) % NX) + q
         return remote(att.at[to], xb.at[t], x_send.at[q, offset], x_recv.at[t], (dp, to))
 
     def x_local():
@@ -252,17 +253,17 @@
         lax.fori_loop(q * 8 // GROUPED, (q + 1) * 8 // GROUPED, attend_some, 0)
         for u in range(4):
             for g in range(8):
-                att[q * 4 + u, :, g * HD : (g + 1) * HD] = attf[
+                att[2 * u + q, :, g * HD : (g + 1) * HD] = attf[
                     q, pl.ds((u * 8 + g) * REQ, REQ), :
                 ].astype(BF16)
         for offset in (2, 1, 3):
             x_copy(q, offset).start()
 
-        @pl.when(t // 4 == q)
+        @pl.when(c == q)
         def _():
             x_local().start()
 
-        @pl.when(t // 4 != q)
+        @pl.when(c != q)
         def _():
             x_copy(q, 0).start()
 
@@ -296,156 +297,181 @@
 
     def y_copy(dx):
         return remote(
-            yb.at[(x + dx) % NX], ab.at[0, x], y_send.at[dx], y_recv.at[x], device(dx=dx)
-        )
-
-    for dx in (2, 1, 3):
-        y_copy(dx).start()
-    pltpu.make_async_copy(yb.at[x], ab.at[0, x], y_recv.at[x]).start()
-
-    def y_arrived(slot):
-        pltpu.make_async_copy(yb.at[0], ab.at[0, slot], y_recv.at[slot]).wait()
-
-    def z_copy(way, d, half):
+            yb.at[(x + dx) % NX], ab.at[0, dx], y_send.at[dx], y_recv.at[dx], device(dx=dx)
+        )
+
+    def z_copy(way, d, k):
         src = 0 if d == 1 else (2 * (d - 1) - 1 if way == 0 else 2 * (d - 1))
         dst = 7 if d == 4 else (2 * d - 1 if way == 0 else 2 * d)
-        rows = pl.ds(2 * half, 2)
         return remote(
-            ab.at[src, rows],
-            ab.at[dst, rows],
-            z_send.at[way, d - 1, half],
-            z_recv.at[way, d - 1, half],
+            ab.at[src, k],
+            ab.at[dst, k],
+            z_send.at[way, d - 1, k],
+            z_recv.at[way, d - 1, k],
             device(dz=1 if way == 0 else NZ - 1),
         )
 
-    def z_first(half):
-        y_arrived(2 * half)
-        y_arrived(2 * half + 1)
-        z_copy(0, 1, half).start()
-        z_copy(1, 1, half).start()
+    def goes(way, d, k):
+        return d < 4 or k // 2 == way
+
+    def z_first(k):
+        if k:
+            y_copy(k).wait_recv()
+        for way in range(2):
+            z_copy(way, 1, k).start()
+
+    ab[0, 0] = yb[x]
+    z_first(0)
+    for dx in (1, 3, 2):
+        y_copy(dx).start()
 
     spans = [(0, 1), (1, 3), (3, 5), (5, 7), (7, 8)]
 
-    def project(stage, i):
+    def slots_of(part):
+        return (0, 4) if part is None else (2 * part, 2 * part + 2)
+
+    def project(stage, part, i):
         lo, hi = spans[stage]
-        rows = (hi - lo) * 64
+        first, last = slots_of(part)
+        rows = (hi - lo) * (last - first) * REQ
         total = jnp.zeros((rows, 256), F32)
         for core in range(2):
-            block = ab[lo:hi, :, core].reshape(rows, 1024)
+            block = ab[lo:hi, first:last, core].reshape(rows, 1024)
             total = total + jnp.dot(block, wb[core, i], preferred_element_type=F32)
-        total = total.astype(BF16).reshape(hi - lo, 64, 256)
-        if i == 0:
-            db[0, lo:hi] = total
-        else:
-            pb[i, lo:hi] = total
-
-    def p_copy(stage, i):
+        total = total.astype(BF16).reshape(hi - lo, (last - first) * REQ, 256)
+        to = pb if i else db
+        to[i, lo:hi, first * REQ : last * REQ] = total
+
+    def p_copy(stage, part, i):
         lo, hi = spans[stage]
-        at = pl.ds(lo, hi - lo)
+        first, last = slots_of(part)
+        at = (i, pl.ds(lo, hi - lo), pl.ds(first * REQ, (last - first) * REQ))
+        n = part or 0
         return remote(
-            pb.at[i, at], db.at[i, at], p_send.at[stage, i], p_recv.at[stage, i], device(dy=i)
+            pb.at[at], db.at[at], p_send.at[stage, n, i], p_recv.at[stage, n, i], device(dy=i)
         )
 
     def z_of(pos):
         dz = 4 if pos == 7 else (NZ - (pos + 1) // 2 if pos % 2 else pos // 2)
         return (z + dz) % NZ
 
-    def e_copy(pos, k):
+    def e_copy(pos, part, k):
         block = z_of(pos)
         to_x = (x + k) % NX
         i = (y + NY - to_x) % NY
+        first, last = slots_of(part)
+        rows = pl.ds(first * REQ, (last - first) * REQ)
         return remote(
-            db.at[i, pos],
-            eb.at[k, c, block % 4],
-            e_send.at[k, pos],
+            db.at[i, pos, rows],
+            eb.at[k, c, block % 4, rows],
+            e_send.at[k, pos, part or 0],
             e_recv.at[k, c, block % 4],
             device(dx=k, core=block // 4),
         )
 
-    def e_local(pos):
+    def e_local(pos, part):
         block = z_of(pos)
         i = (y + NY - x) % NY
+        first, last = slots_of(part)
+        rows = pl.ds(first * REQ, (last - first) * REQ)
         return pltpu.make_async_copy(
-            db.at[i, pos], eb.at[0, c, block % 4], e_recv.at[0, c, block % 4]
-        )
-
-    def forward(stage):
-        for i in (1, 2, 3):
-            p_copy(stage, i).wait_recv()
+            db.at[i, pos, rows], eb.at[0, c, block % 4, rows], e_recv.at[0, c, block % 4]
+        )
+
+    def p_arrived(stage, part):
+        for i in (1, 3, 2):
+            p_copy(stage, part, i).wait_recv()
+
+    def forward(stage, part):
         for pos in range(*spans[stage]):
             for k in (2, 1, 3):
-                e_copy(pos, k).start()
+                e_copy(pos, part, k).start()
             own = z_of(pos) // 4 == c
 
             @pl.when(own)
             def _():
-                e_local(pos).start()
+                e_local(pos, part).start()
 
             @pl.when(jnp.logical_not(own))
             def _():
-                e_copy(pos, 0).start()
-
-    def pass_on(d, half):
+                e_copy(pos, part, 0).start()
+
+    def pass_on(d, k):
         for way in range(2):
-            z_copy(way, d, half).wait_recv()
-            if d < 3 or half == way:
-                z_copy(way, d + 1, half).start()
-
-    def multiply(stage):
-        for i in (1, 3, 2, 0):
-            if stage == 0 and i:
-                w_core(i).wait_recv()
-            project(stage, i)
+            z_copy(way, d, k).wait_recv()
+            if goes(way, d + 1, k):
+                z_copy(way, d + 1, k).start()
+
+    def multiply(stage, part):
+        for i in (2, 1, 3, 0):
+            project(stage, part, i)
             if i:
-                p_copy(stage, i).start()
-
-    z_first(0)
+                p_copy(stage, part, i).start()
+
+    z_first(1)
     w_right[1].wait_recv()
     w_core(3).start()
     w_left[0].wait_recv()
     w_core(1).start()
-    z_first(1)
     pass_on(1, 0)
+    z_first(3)
+    z_first(2)
+    pass_on(1, 1)
+    pass_on(1, 3)
     w_far[0].wait_recv()
     w_far[1].wait_recv()
     w_core(2).start()
-    pass_on(1, 1)
-    w_core(0).wait_recv()
-    multiply(0)
+    for slot in (0, 3, 1):
+        w_core(slot).wait_recv()
+    pass_on(1, 2)
     pass_on(2, 0)
-    multiply(1)
+    w_core(2).wait_recv()
+    multiply(0, None)
     pass_on(2, 1)
-    forward(0)
+    multiply(1, None)
+    pass_on(2, 3)
+    pass_on(2, 2)
     pass_on(3, 0)
-    multiply(2)
-    forward(1)
+    multiply(2, None)
     pass_on(3, 1)
-    multiply(3)
-    forward(2)
-    z_copy(0, 4, 0).wait_recv()
-    z_copy(1, 4, 1).wait_recv()
-    multiply(4)
-    forward(3)
-    forward(4)
+    p_arrived(0, None)
+    forward(0, None)
+    pass_on(3, 3)
+    p_arrived(1, None)
+    forward(1, None)
+    pass_on(3, 2)
+    multiply(3, None)
+    p_arrived(2, None)
+    forward(2, None)
+    for k in (0, 1):
+        z_copy(0, 4, k).wait_recv()
+    for k in (3, 2):
+        z_copy(1, 4, k).wait_recv()
+    multiply(4, None)
+    p_arrived(3, None)
+    forward(3, None)
+    p_arrived(4, None)
+    forward(4, None)
 
     for n in range(1, 5):
         zz = (z + n) % 4
-        rows = pl.ds(pl.multiple_of(zz * REQ, REQ), REQ)
         for core in range(2):
             for k in range(4):
                 pltpu.make_async_copy(
                     db.at[0, 0], eb.at[k, core, zz], e_recv.at[k, core, zz]
                 ).wait()
         for core in range(2):
-            total = eb[0, core, zz].astype(F32)
-            for k in range(1, 4):
-                total = total + eb[k, core, zz].astype(F32)
-            for pair in range(2):
-                for step in range(2):
-                    parts = [total[at : at + 8] for at in (pair * 16 + step * 8, 32 + pair * 16 + step * 8)]
-                    out_ref[4 * pair + 2 * core + step, rows, :] = (
-                        jnp.concatenate(parts, axis=0).astype(BF16)
-                    )
+            for m in range(4):
+                total = eb[0, core, zz, m * REQ : (m + 1) * REQ, :].astype(F32)
+                for k in range(1, 4):
+                    slot = (m - k) % 4
+                    total = total + eb[k, core, zz, slot * REQ : (slot + 1) * REQ, :].astype(F32)
+                source = (x + 4 - m) % 4
+                rows = pl.ds(pl.multiple_of(zz * REQ + core * 8, 8), 8)
+                outf[2 * source, rows, :] = total[:8]
+                outf[2 * source + 1, rows, :] = total[8:]
+    for step in range(STEPS):
+        out_ref[step] = outf[step].astype(BF16)
 
     for copy in w_right + w_left + w_far:
         copy.wait_send()
@@ -455,7 +481,7 @@
         for offset in (1, 2, 3):
             x_copy(q, offset).wait_send()
 
-        @pl.when(t // 4 != q)
+        @pl.when(c != q)
         def _():
             x_copy(q, 0).wait_send()
 
@@ -463,20 +489,22 @@
         y_copy(dx).wait_send()
 
     for d in range(1, 5):
-        for half in range(2):
+        for k in range(4):
             for way in range(2):
-                if d < 4 or half == way:
-                    z_copy(way, d, half).wait_send()
+                if goes(way, d, k):
+                    z_copy(way, d, k).wait_send()
     for stage in range(5):
-        for i in (1, 2, 3):
-            p_copy(stage, i).wait_send()
-    for pos in range(8):
-        for k in (1, 2, 3):
-            e_copy(pos, k).wait_send()
-
-        @pl.when(z_of(pos) // 4 != c)
-        def _():
-            e_copy(pos, 0).wait_send()
+        for part in (None,):
+            for i in (1, 2, 3):
+                p_copy(stage, part, i).wait_send()
+        for pos in range(*spans[stage]):
+            for part in (None,):
+                for k in (1, 2, 3):
+                    e_copy(pos, part, k).wait_send()
+
+                @pl.when(z_of(pos) // 4 != c)
+                def _():
+                    e_copy(pos, part, 0).wait_send()
 
 
 def body(
@@ -510,6 +538,7 @@
             pltpu.VMEM((NY, 8, 64, 256), BF16),
             pltpu.VMEM((NY, 8, 64, 256), BF16),
             pltpu.VMEM((NX, 2, 4, 64, 256), BF16),
+            pltpu.VMEM((STEPS, 64, 256), F32),
             dma((5,)),
             dma((REQ,)),
             dma((REQ,)),
@@ -521,11 +550,11 @@
             dma((8,)),
             dma((4,)),
             dma((4,)),
-            dma((2, 4, 2)),
-            dma((2, 4, 2)),
-            dma((5, 4)),
-            dma((5, 4)),
-            dma((NX, 8)),
+            dma((2, 4, 4)),
+            dma((2, 4, 4)),
+            dma((5, 2, 4)),
+            dma((5, 2, 4)),
+            dma((NX, 8, 2)),
             dma((NX, 2, 4)),
         ],
         compiler_params=pltpu.CompilerParams(

time: 59.7 us -> 58.3 us (0.977)
  Pallas kernels: 57.9 us -> 56.5 us
    pallas_call x1, Pallas kernels: 57.9 us -> 56.5 us  [body(): pl.pallas_call(kernel, out_shape=jax.ShapeDtypeStruct((STEPS, 64, 256), B...]
where the time goes in v3:
time: 58.3 us; the launch traced here: 58.1 us
  Pallas kernels  56.5 us (97%)
  local copies, waits for them, and re-layouts  1.67 us (3%)
    pallas_call x1, Pallas kernels, body(): pl.pallas_call(kernel, out_shape=jax.ShapeDtypeStruct((STEPS, 64, 256), B...  56.5 us
    unnamed x1, local copies, waits for them, and re-layouts  1.67 us

profile of v3, /device:TPU:1, one launch (start us, length us, event | category | flops | bytes accessed | tf_op | source)
XLA Modules:
  0.0 58.1 jit_solution(1556288187422613841)
XLA Ops:
  0.0 56.5 %decode.1 = bf16[8,64,256]{2,1,0:T(8,128)(2,1)} custom-call(s32[16]{0:T(128)} %lengths.1, bf16[8,16,1024]{2,1,0:T(8,128)(2,1)} %q_hbm.1, bf16[8,16,128]{2,1,0:T(8,128)(2,1)} %nk_hbm.1, bf16[8,16,128]{2,1,0:T(8,128)(2,1)} %nv_hbm.1, bf16[16,1,1024,128]{3,2,1,0:T(8,128)(2,1)} %k_hbm.1, bf16[16,1,1024,128]{3,2,1,0:T(8,128)(2,1)} %v_hbm.1, ...), custom_call_target="tpu_custom_call" | custom-call | tf_op jit(solution)/shard_map/decode/pallas_call | solution.py:515
  56.5 1.7 %copy.10 = bf16[8,64,256]{2,1,0:T(8,128)(2,1)} copy(bf16[8,64,256]{2,1,0:T(8,128)(2,1)} %decode.1) | data formatting | bytes 524288

commit v4 on v3

--- a/solution.py
+++ b/solution.py
@@ -431,14 +431,14 @@
     multiply(1, None)
     pass_on(2, 3)
     pass_on(2, 2)
+    multiply(2, None)
     pass_on(3, 0)
-    multiply(2, None)
-    pass_on(3, 1)
     p_arrived(0, None)
     forward(0, None)
-    pass_on(3, 3)
+    pass_on(3, 1)
     p_arrived(1, None)
     forward(1, None)
+    pass_on(3, 3)
     pass_on(3, 2)
     multiply(3, None)
     p_arrived(2, None)

time: 58.3 us -> 58.3 us (level)
  no operation moved by 1% of the time
where the time goes in v4:
time: 58.3 us; the launch traced here: 58.1 us
  Pallas kernels  56.5 us (97%)
  local copies, waits for them, and re-layouts  1.67 us (3%)
    pallas_call x1, Pallas kernels, body(): pl.pallas_call(kernel, out_shape=jax.ShapeDtypeStruct((STEPS, 64, 256), B...  56.5 us
    unnamed x1, local copies, waits for them, and re-layouts  1.67 us

profile of v4, /device:TPU:1, one launch (start us, length us, event | category | flops | bytes accessed | tf_op | source)
XLA Modules:
  0.0 58.1 jit_solution(6923186780537100044)
XLA Ops:
  0.0 56.5 %decode.1 = bf16[8,64,256]{2,1,0:T(8,128)(2,1)} custom-call(s32[16]{0:T(128)} %lengths.1, bf16[8,16,1024]{2,1,0:T(8,128)(2,1)} %q_hbm.1, bf16[8,16,128]{2,1,0:T(8,128)(2,1)} %nk_hbm.1, bf16[8,16,128]{2,1,0:T(8,128)(2,1)} %nv_hbm.1, bf16[16,1,1024,128]{3,2,1,0:T(8,128)(2,1)} %k_hbm.1, bf16[16,1,1024,128]{3,2,1,0:T(8,128)(2,1)} %v_hbm.1, ...), custom_call_target="tpu_custom_call" | custom-call | tf_op jit(solution)/shard_map/decode/pallas_call | solution.py:515
  56.5 1.7 %copy.10 = bf16[8,64,256]{2,1,0:T(8,128)(2,1)} copy(bf16[8,64,256]{2,1,0:T(8,128)(2,1)} %decode.1) | data formatting | bytes 524288
